TPU v7x, 32 devices: a whole 2x2x4 slice. The times are simulated.
32 devices in a mesh: fsdp: 16 (over z, y, x), dp: 2 (over core).
Axes of the slice: x: 2, y: 2, z: 4, core: 2. Of those that a mesh axis runs over, the one named last changes fastest.
Arguments:
- tokens: bfloat16 [32, 1024, 768], P(('fsdp', 'dp')), may hold values from -16 to 16
- segment_ids: int32 [32, 1024], P(('fsdp', 'dp')), may hold values from 0 to 8, as said below
- cotangent: bfloat16 [32, 1024, 768], P(('fsdp', 'dp')), may hold values from -6 to 6
- weight_query: bfloat16 [768, 768], P(None, 'fsdp'), may hold values from -0.21875 to 0.21875
- weight_key: bfloat16 [768, 768], P(None, 'fsdp'), may hold values from -0.21875 to 0.21875
- weight_value: bfloat16 [768, 768], P(None, 'fsdp'), may hold values from -0.21875 to 0.21875
- weight_output: bfloat16 [768, 768], P(None, 'fsdp'), may hold values from -2.5 to 2.5
- weight_inner: bfloat16 [768, 3072], P(None, 'fsdp'), may hold values from -0.21875 to 0.21875
- weight_outer: bfloat16 [3072, 768], P(None, 'fsdp'), may hold values from -0.109375 to 0.109375
- bias_query: bfloat16 [768], P('fsdp'), may hold values from -3 to 3
- bias_value: bfloat16 [768], P('fsdp'), may hold values from -3 to 3
- bias_output: bfloat16 [768], P('fsdp'), may hold values from -3 to 3
- bias_inner: bfloat16 [3072], P('fsdp'), may hold values from -3 to 3
- bias_outer: bfloat16 [768], P('fsdp'), may hold values from -3 to 3
- gain_attn: bfloat16 [768], P('fsdp'), may hold values from 0.5 to 1.5
- shift_attn: bfloat16 [768], P('fsdp'), may hold values from -2 to 2
- gain_ffn: bfloat16 [768], P('fsdp'), may hold values from 0.5 to 1.5
- shift_ffn: bfloat16 [768], P('fsdp'), may hold values from -2 to 2
Outputs:
- output: bfloat16 [32, 1024, 768], P(('fsdp', 'dp'))
- grad_tokens: bfloat16 [32, 1024, 768], P(('fsdp', 'dp'))
- grad_weight_query: float32 [768, 768], P(None, 'fsdp')
- grad_weight_key: float32 [768, 768], P(None, 'fsdp')
- grad_weight_value: float32 [768, 768], P(None, 'fsdp')
- grad_weight_output: float32 [768, 768], P(None, 'fsdp')
- grad_weight_inner: float32 [768, 3072], P(None, 'fsdp')
- grad_weight_outer: float32 [3072, 768], P(None, 'fsdp')
- grad_bias_query: float32 [768], P('fsdp')
- grad_bias_value: float32 [768], P('fsdp')
- grad_bias_output: float32 [768], P('fsdp')
- grad_bias_inner: float32 [3072], P('fsdp')
- grad_bias_outer: float32 [768], P('fsdp')
- grad_gain_attn: float32 [768], P('fsdp')
- grad_shift_attn: float32 [768], P('fsdp')
- grad_gain_ffn: float32 [768], P('fsdp')
- grad_shift_ffn: float32 [768], P('fsdp')
- rms_stats: float32 [4], replicated
Inputs may be any that keep to these rules, and one draw needn't show every extreme that they name: `segment_ids`: within each sequence the ids start at 1 on its first token, never fall and grow by one at each new document; a new document begins at least at every multiple of 128 positions until the id reaches 8, after which the rest of the sequence is one document; 0 marks padding, which fills only a sequence's end.
All inputs are finite; a program needn't handle non-finite values.
Results may differ from a plain program's by a relative error of at most 0.013.
Values may be sent and summed in bfloat16 or wider, within the bound.
A program may use at most 192 MiB of HBM per device.

v0:
```python
import math

import jax
import jax.numpy as jnp
from jax import lax
from jax.sharding import PartitionSpec as P

HD = 64


def scaled(values, gain_vec):
    average = jnp.mean(values, axis=-1, keepdims=True)
    centered = values - average
    spread = jnp.mean(centered * centered, axis=-1, keepdims=True)
    return centered * lax.rsqrt(spread + 1e-06) * gain_vec


def matmul(operand, matrix):
    return jnp.dot(operand, matrix, preferred_element_type=jnp.float32)


def over_rows(operand, other):
    return lax.dot_general(
        operand, other, (((0,), (0,)), ((), ())), preferred_element_type=jnp.float32
    )


def against(operand, matrix):
    return lax.dot_general(
        operand, matrix, (((1,), (1,)), ((), ())), preferred_element_type=jnp.float32
    )


def pair_of(block, offset, seq_len):
    return lax.dynamic_slice_in_dim(block, offset, 2 * HD, 1).reshape(seq_len, 2, HD)


def masked_scores(query_pair, key_pair, same_doc, factor):
    scores = (
        jnp.einsum("qhd,khd->hqk", query_pair, key_pair, preferred_element_type=jnp.float32)
        * factor
    )
    return jnp.where(same_doc, scores, -1e30)


def attend_forward(queries, key_rows, value_rows, doc_ids):
    seq_len, features = queries.shape
    pair_width = 2 * HD
    factor = 1.0 / math.sqrt(HD)
    same_doc = (doc_ids[:, None] == doc_ids[None, :])[None]

    def one_pair(which, buffers):
        attended, logsum = buffers
        offset = which * pair_width
        query_pair = pair_of(queries, offset, seq_len)
        key_pair = pair_of(key_rows, offset, seq_len)
        value_pair = pair_of(value_rows, offset, seq_len)
        scores = masked_scores(query_pair, key_pair, same_doc, factor)
        largest = jnp.max(scores, axis=-1, keepdims=True)
        exponent = jnp.exp(scores - largest)
        denominator = jnp.sum(exponent, axis=-1, keepdims=True)
        probability = (exponent / denominator).astype(jnp.bfloat16)
        mixed_pair = jnp.einsum(
            "hqk,khd->qhd", probability, value_pair, preferred_element_type=jnp.float32
        )
        attended = lax.dynamic_update_slice_in_dim(
            attended, mixed_pair.reshape(seq_len, pair_width), offset, 1
        )
        logsum = lax.dynamic_update_slice_in_dim(
            logsum, (largest + jnp.log(denominator))[:, :, 0], which * 2, 0
        )
        return (attended, logsum)

    initial = (
        jnp.zeros((seq_len, features), jnp.float32),
        jnp.zeros((features // HD, seq_len), jnp.float32),
    )
    return lax.fori_loop(0, features // pair_width, one_pair, initial)


def attend_backward(queries, key_rows, value_rows, upstream, logsum, doc_ids):
    seq_len, features = queries.shape
    pair_width = 2 * HD
    factor = 1.0 / math.sqrt(HD)
    same_doc = (doc_ids[:, None] == doc_ids[None, :])[None]

    def one_pair(which, buffers):
        grad_queries, grad_keys, grad_values = buffers
        offset = which * pair_width
        query_pair = pair_of(queries, offset, seq_len)
        key_pair = pair_of(key_rows, offset, seq_len)
        value_pair = pair_of(value_rows, offset, seq_len)
        upper_pair = pair_of(upstream, offset, seq_len)
        logsum_pair = lax.dynamic_slice_in_dim(logsum, which * 2, 2, 0)
        scores = masked_scores(query_pair, key_pair, same_doc, factor)
        probability = jnp.exp(scores - logsum_pair[:, :, None])
        rounded = probability.astype(jnp.bfloat16)
        value_part = jnp.einsum(
            "hqk,qhd->khd", rounded, upper_pair, preferred_element_type=jnp.float32
        )
        prob_grad = jnp.einsum(
            "qhd,khd->hqk", upper_pair, value_pair, preferred_element_type=jnp.float32
        )
        weighted = jnp.sum(probability * prob_grad, axis=-1, keepdims=True)
        score_grad = (probability * (prob_grad - weighted)).astype(jnp.bfloat16)
        query_part = (
            jnp.einsum("hqk,khd->qhd", score_grad, key_pair, preferred_element_type=jnp.float32)
            * factor
        )
        key_part = (
            jnp.einsum("hqk,qhd->khd", score_grad, query_pair, preferred_element_type=jnp.float32)
            * factor
        )
        grad_queries = lax.dynamic_update_slice_in_dim(
            grad_queries, query_part.reshape(seq_len, pair_width), offset, 1
        )
        grad_keys = lax.dynamic_update_slice_in_dim(
            grad_keys, key_part.reshape(seq_len, pair_width), offset, 1
        )
        grad_values = lax.dynamic_update_slice_in_dim(
            grad_values, value_part.reshape(seq_len, pair_width), offset, 1
        )
        return (grad_queries, grad_keys, grad_values)

    empty_buf = jnp.zeros((seq_len, features), jnp.float32)
    return lax.fori_loop(0, features // pair_width, one_pair, (empty_buf, empty_buf, empty_buf))


def body(
    tokens,
    segment_ids,
    cotangent,
    weight_query,
    weight_key,
    weight_value,
    weight_output,
    weight_inner,
    weight_outer,
    bias_query,
    bias_value,
    bias_output,
    bias_inner,
    bias_outer,
    gain_attn,
    shift_attn,
    gain_ffn,
    shift_ffn,
):
    gathered = (
        lax.all_gather(weight_query, "fsdp", axis=1, tiled=True),
        lax.all_gather(weight_key, "fsdp", axis=1, tiled=True),
        lax.all_gather(weight_value, "fsdp", axis=1, tiled=True),
        lax.all_gather(weight_output, "fsdp", axis=1, tiled=True),
        lax.all_gather(weight_inner, "fsdp", axis=1, tiled=True),
        lax.all_gather(weight_outer, "fsdp", axis=1, tiled=True),
        lax.all_gather(bias_query, "fsdp", axis=0, tiled=True),
        lax.all_gather(bias_value, "fsdp", axis=0, tiled=True),
        lax.all_gather(bias_output, "fsdp", axis=0, tiled=True),
        lax.all_gather(bias_inner, "fsdp", axis=0, tiled=True),
        lax.all_gather(bias_outer, "fsdp", axis=0, tiled=True),
        lax.all_gather(gain_attn, "fsdp", axis=0, tiled=True),
        lax.all_gather(shift_attn, "fsdp", axis=0, tiled=True),
        lax.all_gather(gain_ffn, "fsdp", axis=0, tiled=True),
        lax.all_gather(shift_ffn, "fsdp", axis=0, tiled=True),
    )
    (
        whole_query,
        whole_key,
        whole_value,
        whole_output,
        whole_inner,
        whole_outer,
        query_bias,
        value_bias,
        output_bias,
        inner_bias,
        outer_bias,
        attn_gain,
        attn_shift,
        ffn_gain,
        ffn_shift,
    ) = gathered
    count_seq, seq_len, features = tokens.shape
    row_count = count_seq * seq_len
    stream = tokens.reshape(row_count, features).astype(jnp.float32)
    normed = (
        scaled(stream, attn_gain.astype(jnp.float32)) + attn_shift.astype(jnp.float32)
    ).astype(jnp.bfloat16)
    queries = (matmul(normed, whole_query) + query_bias.astype(jnp.float32)).astype(jnp.bfloat16)
    key_rows = matmul(normed, whole_key).astype(jnp.bfloat16)
    value_rows = (matmul(normed, whole_value) + value_bias.astype(jnp.float32)).astype(jnp.bfloat16)
    query_seq = queries.reshape(count_seq, seq_len, features)
    key_seq = key_rows.reshape(count_seq, seq_len, features)
    value_seq = value_rows.reshape(count_seq, seq_len, features)
    attended, logsum = lax.map(
        lambda packed: attend_forward(*packed), (query_seq, key_seq, value_seq, segment_ids)
    )
    attended = attended.reshape(row_count, features).astype(jnp.bfloat16)
    branch = matmul(attended, whole_output) + output_bias.astype(jnp.float32)
    middle = stream + branch
    second = (scaled(middle, ffn_gain.astype(jnp.float32)) + ffn_shift.astype(jnp.float32)).astype(
        jnp.bfloat16
    )
    hidden = matmul(second, whole_inner) + inner_bias.astype(jnp.float32)
    active = jax.nn.gelu(hidden, approximate=False).astype(jnp.bfloat16)
    ffn_out = matmul(active, whole_outer) + outer_bias.astype(jnp.float32)
    result = middle + ffn_out
    valid_mask = (segment_ids != 0).reshape(row_count).astype(jnp.float32)
    squares = jnp.stack(
        [
            jnp.sum(jnp.sum(piece * piece, axis=-1) * valid_mask)
            for piece in (stream, branch, middle, ffn_out)
        ]
    )
    counted = jnp.sum(valid_mask)
    regathered = (
        lax.all_gather(weight_query, "fsdp", axis=1, tiled=True),
        lax.all_gather(weight_key, "fsdp", axis=1, tiled=True),
        lax.all_gather(weight_value, "fsdp", axis=1, tiled=True),
        lax.all_gather(weight_output, "fsdp", axis=1, tiled=True),
        lax.all_gather(weight_inner, "fsdp", axis=1, tiled=True),
        lax.all_gather(weight_outer, "fsdp", axis=1, tiled=True),
        lax.all_gather(gain_attn, "fsdp", axis=0, tiled=True),
        lax.all_gather(gain_ffn, "fsdp", axis=0, tiled=True),
    )
    (
        back_query,
        back_key,
        back_value,
        back_output,
        back_inner,
        back_outer,
        back_attn_gain,
        back_ffn_gain,
    ) = regathered
    grad_out = cotangent.reshape(row_count, features)
    grad_outer = over_rows(active, grad_out)
    biasgrad_outer = jnp.sum(grad_out.astype(jnp.float32), axis=0)
    grad_active = against(grad_out, back_outer)
    _, gelu_back = jax.vjp(lambda values: jax.nn.gelu(values, approximate=False), hidden)
    grad_hidden = gelu_back(grad_active)[0].astype(jnp.bfloat16)
    grad_inner = over_rows(second, grad_hidden)
    biasgrad_inner = jnp.sum(grad_hidden.astype(jnp.float32), axis=0)
    grad_second = against(grad_hidden, back_inner)
    _, norm_back_ffn = jax.vjp(scaled, middle, back_ffn_gain.astype(jnp.float32))
    grad_middle, gaingrad_ffn = norm_back_ffn(grad_second)
    shiftgrad_ffn = jnp.sum(grad_second, axis=0)
    grad_middle = grad_middle + grad_out.astype(jnp.float32)
    grad_branch = grad_middle.astype(jnp.bfloat16)
    grad_output = over_rows(attended, grad_branch)
    biasgrad_output = jnp.sum(grad_branch.astype(jnp.float32), axis=0)
    grad_attended = against(grad_branch, back_output).astype(jnp.bfloat16)
    upstream_seq = grad_attended.reshape(count_seq, seq_len, features)
    grad_q_seq, grad_k_seq, grad_v_seq = lax.map(
        lambda packed: attend_backward(*packed),
        (query_seq, key_seq, value_seq, upstream_seq, logsum, segment_ids),
    )
    grad_queries = grad_q_seq.reshape(row_count, features).astype(jnp.bfloat16)
    grad_keys = grad_k_seq.reshape(row_count, features).astype(jnp.bfloat16)
    grad_values = grad_v_seq.reshape(row_count, features).astype(jnp.bfloat16)
    grad_query = over_rows(normed, grad_queries)
    grad_key = over_rows(normed, grad_keys)
    grad_value = over_rows(normed, grad_values)
    biasgrad_query = jnp.sum(grad_queries.astype(jnp.float32), axis=0)
    biasgrad_value = jnp.sum(grad_values.astype(jnp.float32), axis=0)
    grad_normed = (
        against(grad_queries, back_query)
        + against(grad_keys, back_key)
        + against(grad_values, back_value)
    )
    _, norm_back_attn = jax.vjp(scaled, stream, back_attn_gain.astype(jnp.float32))
    grad_stream, gaingrad_attn = norm_back_attn(grad_normed)
    shiftgrad_attn = jnp.sum(grad_normed, axis=0)
    grad_input = (grad_middle + grad_stream).astype(jnp.bfloat16).reshape(tokens.shape)
    square_total, count_total = lax.psum((squares, counted), ("fsdp", "dp"))
    reduced = (
        lax.psum_scatter(grad_query, "fsdp", scatter_dimension=1, tiled=True),
        lax.psum_scatter(grad_key, "fsdp", scatter_dimension=1, tiled=True),
        lax.psum_scatter(grad_value, "fsdp", scatter_dimension=1, tiled=True),
        lax.psum_scatter(grad_output, "fsdp", scatter_dimension=1, tiled=True),
        lax.psum_scatter(grad_inner, "fsdp", scatter_dimension=1, tiled=True),
        lax.psum_scatter(grad_outer, "fsdp", scatter_dimension=1, tiled=True),
        lax.psum_scatter(biasgrad_query, "fsdp", scatter_dimension=0, tiled=True),
        lax.psum_scatter(biasgrad_value, "fsdp", scatter_dimension=0, tiled=True),
        lax.psum_scatter(biasgrad_output, "fsdp", scatter_dimension=0, tiled=True),
        lax.psum_scatter(biasgrad_inner, "fsdp", scatter_dimension=0, tiled=True),
        lax.psum_scatter(biasgrad_outer, "fsdp", scatter_dimension=0, tiled=True),
        lax.psum_scatter(gaingrad_attn, "fsdp", scatter_dimension=0, tiled=True),
        lax.psum_scatter(shiftgrad_attn, "fsdp", scatter_dimension=0, tiled=True),
        lax.psum_scatter(gaingrad_ffn, "fsdp", scatter_dimension=0, tiled=True),
        lax.psum_scatter(shiftgrad_ffn, "fsdp", scatter_dimension=0, tiled=True),
    )
    summed = (
        lax.psum(reduced[0].astype(jnp.bfloat16), "dp").astype(jnp.float32),
        lax.psum(reduced[1].astype(jnp.bfloat16), "dp").astype(jnp.float32),
        lax.psum(reduced[2].astype(jnp.bfloat16), "dp").astype(jnp.float32),
        lax.psum(reduced[3].astype(jnp.bfloat16), "dp").astype(jnp.float32),
        lax.psum(reduced[4].astype(jnp.bfloat16), "dp").astype(jnp.float32),
        lax.psum(reduced[5].astype(jnp.bfloat16), "dp").astype(jnp.float32),
        lax.psum(reduced[6].astype(jnp.bfloat16), "dp").astype(jnp.float32),
        lax.psum(reduced[7].astype(jnp.bfloat16), "dp").astype(jnp.float32),
        lax.psum(reduced[8].astype(jnp.bfloat16), "dp").astype(jnp.float32),
        lax.psum(reduced[9].astype(jnp.bfloat16), "dp").astype(jnp.float32),
        lax.psum(reduced[10].astype(jnp.bfloat16), "dp").astype(jnp.float32),
        lax.psum(reduced[11].astype(jnp.bfloat16), "dp").astype(jnp.float32),
        lax.psum(reduced[12].astype(jnp.bfloat16), "dp").astype(jnp.float32),
        lax.psum(reduced[13].astype(jnp.bfloat16), "dp").astype(jnp.float32),
        lax.psum(reduced[14].astype(jnp.bfloat16), "dp").astype(jnp.float32),
    )
    rms_stats = jnp.sqrt(square_total / (count_total * features))
    return (
        result.astype(jnp.bfloat16).reshape(tokens.shape),
        grad_input,
        summed[0],
        summed[1],
        summed[2],
        summed[3],
        summed[4],
        summed[5],
        summed[6],
        summed[7],
        summed[8],
        summed[9],
        summed[10],
        summed[11],
        summed[12],
        summed[13],
        summed[14],
        rms_stats,
    )


def solution(mesh):
    in_specs = (
        P(("fsdp", "dp"), None, None),
        P(("fsdp", "dp"), None),
        P(("fsdp", "dp"), None, None),
        P(None, "fsdp"),
        P(None, "fsdp"),
        P(None, "fsdp"),
        P(None, "fsdp"),
        P(None, "fsdp"),
        P(None, "fsdp"),
        P("fsdp"),
        P("fsdp"),
        P("fsdp"),
        P("fsdp"),
        P("fsdp"),
        P("fsdp"),
        P("fsdp"),
        P("fsdp"),
        P("fsdp"),
    )
    out_specs = (
        P(("fsdp", "dp"), None, None),
        P(("fsdp", "dp"), None, None),
        P(None, "fsdp"),
        P(None, "fsdp"),
        P(None, "fsdp"),
        P(None, "fsdp"),
        P(None, "fsdp"),
        P(None, "fsdp"),
        P("fsdp"),
        P("fsdp"),
        P("fsdp"),
        P("fsdp"),
        P("fsdp"),
        P("fsdp"),
        P("fsdp"),
        P("fsdp"),
        P("fsdp"),
        P(),
    )
    return jax.shard_map(body, mesh=mesh, in_specs=in_specs, out_specs=out_specs, check_vma=False)
```

profile of v0, /device:TPU:0, one launch (start us, length us, event | category | flops | bytes accessed | tf_op | source)
XLA Modules:
  0.0 1517.3 jit_solution(17523102741560861329)
XLA Ops:
  21.4 79.0 %all-reduce.20 = (bf16[768]{0:T(1024)(128)(2,1)S(1)}, bf16[768]{0:T(1024)(128)(2,1)S(1)}, bf16[768]{0:T(1024)(128)(2,1)S(1)}, bf16[768]{0:T(1024)(128)(2,1)S(1)}...) all-reduce(bf16[768]{0:T(1024)(128)(2,1)S(1)} %dynamic-update-slice, ...), channel_id=1, replica_groups=mesh['fsdp'=16,'dp'=2] {'fsdp'}, use_global_device_ids=true, to_apply=%add.2 | all-reduce | flops 9216 | bytes 36864
  110.6 17.1 %all-gather.7.cloned.1.call-done = bf16[768,768]{0,1:T(8,128)(2,1)} async-done(((bf16[768,48]{0,1:T(8,128)(2,1)}), bf16[768,768]{0,1:T(8,128)(2,1)}) %all-gather.7.cloned.1.call-update) | async-done | bytes 1179664 | tf_op jit(solution)/shard_map/all_gather | solution.py:152
  132.4 53.2 %all-gather.11.cloned.1.call-done = bf16[768,768]{0,1:T(8,128)(2,1)} async-done(((bf16[768,48]{0,1:T(8,128)(2,1)}), bf16[768,768]{0,1:T(8,128)(2,1)}) %all-gather.11.cloned.1.call-update) | async-done | bytes 1179664 | tf_op jit(solution)/shard_map/all_gather | solution.py:151
  193.7 94.6 %while.54 = (s32[]{:T(128)}, bf16[1024,768]{0,1:T(8,128)(2,1)}, f32[12,1024]{1,0:T(8,128)S(1)}, bf16[1024,768]{0,1:T(8,128)(2,1)}, bf16[1024,768]{0,1:T(8,128)(2...) while((s32[]{:T(128)}, bf16[1024,768]{0,1:T(8,128)(2,1)}, ...), condition=%wide.region_5.6_spmd.clone, body=%wide.region_2.5_spmd.clone.sunk | while | flops 563083264 | bytes 66130180 | solution.py:78
  204.0 5.1 fusion.146
  219.7 5.1 fusion.146
  235.3 5.1 fusion.146
  251.0 5.2 fusion.146
  282.4 5.1 fusion.146
  294.3 30.8 %all-gather.15.cloned.1.call-done = bf16[768,3072]{0,1:T(8,128)(2,1)} async-done(((bf16[768,192]{0,1:T(8,128)(2,1)}), bf16[768,3072]{0,1:T(8,128)(2,1)}) %all-gather.15.cloned.1.call-update) | async-done | bytes 4718608 | tf_op jit(solution)/shard_map/all_gather | solution.py:154
  325.1 37.9 %multiply_convert_fusion.1 = (bf16[1024,3072]{1,0:T(8,128)(2,1)}, f32[1024,3072]{1,0:T(8,128)}, f32[1024,3072]{1,0:T(8,128)}) fusion(f32[3072]{0:T(1024)S(1)} %convert_element_type.238, bf16[768,3072]{0,1:T(8,128)(2,1)} %all-gather.15.cloned.1.call-done, f32[1024,768]{0,1:T(8,128)} %copy-done.7, f32[768]{0:T(1024)S(1)} %convert_element_type.236, ...), kind=kOutput, calls=%fused_computation.39 | convolution fusion | flops 5043388416 | bytes 39348224 | tf_op jit(solution)/shard_map/dot_general | solution.py:19
  363.0 44.0 %all-gather.17.cloned.1.call-done = bf16[3072,768]{0,1:T(8,128)(2,1)} async-done(((bf16[3072,48]{0,1:T(8,128)(2,1)}), bf16[3072,768]{0,1:T(8,128)(2,1)}) %all-gather.17.cloned.1.call-update) | async-done | bytes 4718608 | tf_op jit(solution)/shard_map/all_gather | solution.py:155
  407.0 17.4 %convert_reduce_fusion = (f32[3072]{0:T(1024)}, bf16[1024,3072]{1,0:T(8,128)(2,1)}) fusion(f32[1024,3072]{1,0:T(8,128)} %get-tuple-element.588, bf16[3072,768]{0,1:T(8,128)(2,1)} %all-gather.17.cloned.1.call-done, bf16[1,1024,768]{2,1,0:T(8,128)(2,1)S(1)} %copy-done.14, f32[1024,3072]{1,0:T(8,128)} %get-tuple-element.608, f32[3072]{0:T(1024)S(1)} %convert_element_type.238), kind=kOutput, calls=%fused_computation.37 | convolution fusion | flops 4885312512 | bytes 37773312 | tf_op jit(solution)/shard_map/dot_general | solution.py:29
  424.5 9.1 fusion.80
  441.0 11.1 multiply_reduce_fusion.1
  464.8 148.6 %while.55 = (s32[]{:T(128)}, bf16[1024,768]{0,1:T(8,128)(2,1)}, bf16[1024,768]{0,1:T(8,128)(2,1)}, bf16[1024,768]{0,1:T(8,128)(2,1)}, bf16[1024,768]{0,1:T(8,128...) while((s32[]{:T(128)}, bf16[1024,768]{0,1:T(8,128)(2,1)}, ...), condition=%wide.region_12.13_spmd.clone, body=%wide.region_10.12_spmd.clone.sunk | while | flops 1375205376 | bytes 99152184 | solution.py:126
  475.4 5.6 multiply_reduce_fusion.8
  500.1 5.6 multiply_reduce_fusion.8
  524.8 5.6 multiply_reduce_fusion.8
  549.5 5.6 multiply_reduce_fusion.8
  574.2 5.6 multiply_reduce_fusion.8
  598.8 5.6 multiply_reduce_fusion.8
  625.8 11.0 fusion.65
  636.9 10.0 fusion.44
  663.7 81.5 %reduce-scatter.7.cloned.1.call-done = f32[768,48]{0,1:T(8,128)} async-done(((f32[768,768]{0,1:T(8,128)}), f32[768,48]{0,1:T(8,128)}) %reduce-scatter.7.cloned.1.call-update) | async-done | bytes 147472 | tf_op jit(solution)/shard_map/reduce_scatter | solution.py:277
  746.7 130.8 %reduce-scatter.9.cloned.1.call-done = f32[768,48]{0,1:T(8,128)} async-done(((f32[768,768]{0,1:T(8,128)}), f32[768,48]{0,1:T(8,128)}) %reduce-scatter.9.cloned.1.call-update) | async-done | bytes 147472 | tf_op jit(solution)/shard_map/reduce_scatter | solution.py:278
  879.1 131.4 %reduce-scatter.11.cloned.1.call-done = f32[768,48]{0,1:T(8,128)} async-done(((f32[768,768]{0,1:T(8,128)}), f32[768,48]{0,1:T(8,128)}) %reduce-scatter.11.cloned.1.call-update) | async-done | bytes 147472 | tf_op jit(solution)/shard_map/reduce_scatter | solution.py:279
  1012.1 173.6 %reduce-scatter.15.cloned.1.call-done = f32[768,192]{0,1:T(8,128)} async-done(((f32[768,3072]{0,1:T(8,128)}), f32[768,192]{0,1:T(8,128)}) %reduce-scatter.15.cloned.1.call-update) | async-done | bytes 589840 | tf_op jit(solution)/shard_map/reduce_scatter | solution.py:281
  1187.4 174.8 %reduce-scatter.17.cloned.1.call-done = f32[3072,48]{0,1:T(8,128)} async-done(((f32[3072,768]{0,1:T(8,128)}), f32[3072,48]{0,1:T(8,128)}) %reduce-scatter.17.cloned.1.call-update) | async-done | bytes 589840 | tf_op jit(solution)/shard_map/reduce_scatter | solution.py:282
  1366.7 39.3 %all-reduce.18 = (f32[4]{0:T(128)S(1)}, f32[]{:T(128)}) all-reduce(f32[4]{0:T(128)S(1)} %pad_maximum_fusion, f32[]{:T(128)} %get-tuple-element.509), channel_id=1, replica_groups=mesh['fsdp'=16,'dp'=2] {'fsdp','dp'}, use_global_device_ids=true, to_apply=%region_62.63 | all-reduce | flops 5 | bytes 40 | tf_op jit(solution)/shard_map/psum | solution.py:275
  1406.1 5.5 convert_reduce_fusion.2
  1411.7 75.9 %all-reduce.19 = (bf16[768]{0:T(1024)(128)(2,1)S(1)}, bf16[768]{0:T(1024)(128)(2,1)S(1)}, bf16[768]{0:T(1024)(128)(2,1)S(1)}, bf16[3072]{0:T(1024)(128)(2,1)S(1)...) all-reduce(f32[768]{0:T(1024)S(1)} %get-tuple-element.615, ...), channel_id=8, replica_groups=mesh['fsdp'=16,'dp'=2] {'fsdp'}, use_global_device_ids=true, to_apply=%region_28.29.clone | all-reduce | flops 9216 | bytes 55296
  (386 shorter events, 305.1 us)
Async XLA Ops:
  7.2 98.8 %all-gather.9.cloned.1.call-start = ((), (), s32[]{:S(2)}) async-start(), calls=%async_computation.7 | async-start | bytes 1253376 | tf_op jit(solution)/shard_map/all_gather | solution.py:150
  7.9 119.8 %all-gather.7.cloned.1.call-start = ((), (), s32[]{:S(2)}) async-start(), calls=%async_computation.6 | async-start | bytes 1253376 | tf_op jit(solution)/shard_map/all_gather | solution.py:152
  8.7 176.9 %all-gather.11.cloned.1.call-start = ((), (), s32[]{:S(2)}) async-start(), calls=%async_computation.8 | async-start | bytes 1253376 | tf_op jit(solution)/shard_map/all_gather | solution.py:151
  9.4 278.9 %all-gather.13.cloned.1.call-start = ((), (), s32[]{:S(2)}) async-start(), calls=%async_computation.9 | async-start | bytes 1253376 | tf_op jit(solution)/shard_map/all_gather | solution.py:153
  10.0 315.1 %all-gather.15.cloned.1.call-start = ((), (), s32[]{:S(2)}) async-start(), calls=%async_computation.10 | async-start | bytes 5013504 | tf_op jit(solution)/shard_map/all_gather | solution.py:154
  10.6 396.4 %all-gather.17.cloned.1.call-start = ((), (), s32[]{:S(2)}) async-start(), calls=%async_computation.11 | async-start | bytes 5013504 | tf_op jit(solution)/shard_map/all_gather | solution.py:155
  11.1 650.9 %reduce-scatter.13.cloned.1.call-start = ((), (), s32[]{:S(2)}) async-start(), calls=%async_computation.15 | async-start | bytes 2506752 | tf_op jit(solution)/shard_map/reduce_scatter | solution.py:280
  100.4 85.1 %copy-start.20 = (f32[768]{0:T(1024)}, f32[768]{0:T(1024)S(1)}, u32[]{:S(2)}) copy-start(f32[768]{0:T(1024)S(1)} %convert_element_type.225) | copy-start | bytes 9220
  100.4 85.1 %copy-start.34 = (f32[768]{0:T(1024)}, f32[768]{0:T(1024)S(1)}, u32[]{:S(2)}) copy-start(f32[768]{0:T(1024)S(1)} %convert_element_type.226) | copy-start | bytes 9220
  102.3 186.0 %copy-start.1 = (bf16[1,1024,768]{1,2,0:T(8,128)(2,1)}, bf16[1,1024,768]{1,2,0:T(8,128)(2,1)S(1)}, u32[]{:S(2)}) copy-start(bf16[1,1024,768]{1,2,0:T(8,128)(2,1)S(1)} %copy.60) | copy-start | bytes 4718596
  102.6 83.0 %copy-start.17 = (f32[1024]{0:T(1024)}, f32[1024]{0:T(1024)S(1)}, u32[]{:S(2)}) copy-start(f32[1024]{0:T(1024)S(1)} %broadcast_multiply_fusion.1) | copy-start | bytes 12292
  103.6 81.9 %copy-start.22 = (f32[1024]{0:T(1024)}, f32[1024]{0:T(1024)S(1)}, u32[]{:S(2)}) copy-start(f32[1024]{0:T(1024)S(1)} %fusion.56) | copy-start | bytes 12292
  103.7 221.4 %copy-start.36 = (f32[768]{0:T(1024)}, f32[768]{0:T(1024)S(1)}, u32[]{:S(2)}) copy-start(f32[768]{0:T(1024)S(1)} %convert_element_type.236) | copy-start | bytes 9220
  294.3 112.8 %copy-start.14 = (bf16[1,1024,768]{2,1,0:T(8,128)(2,1)S(1)}, bf16[1,1024,768]{2,1,0:T(8,128)(2,1)}, u32[]{:S(2)}) copy-start(bf16[1,1024,768]{2,1,0:T(8,128)(2,1)} %param.24) | copy-start | bytes 4718596
  407.0 17.4 %copy-start.40 = (bf16[768,3072]{0,1:T(8,128)(2,1)S(1)}, bf16[768,3072]{0,1:T(8,128)(2,1)}, u32[]{:S(2)}) copy-start(bf16[768,3072]{0,1:T(8,128)(2,1)} %all-gather.15.cloned.1.call-done) | copy-start | bytes 14155780
  441.0 11.1 copy-start.5
  458.1 287.1 %reduce-scatter.7.cloned.1.call-start = ((), (), s32[]{:S(2)}) async-start(), calls=%async_computation.12 | async-start | bytes 2506752 | tf_op jit(solution)/shard_map/reduce_scatter | solution.py:277
  464.8 148.7 %copy-start.2 = (bf16[1,1024,768]{1,2,0:T(8,128)(2,1)S(1)}, bf16[1,1024,768]{1,2,0:T(8,128)(2,1)}, u32[]{:S(2)}) copy-start(bf16[1,1024,768]{1,2,0:T(8,128)(2,1)} %copy-done.1) | copy-start | bytes 4718596
  464.8 148.7 %copy-start.18 = (f32[1024]{0:T(1024)S(1)}, f32[1024]{0:T(1024)}, u32[]{:S(2)}) copy-start(f32[1024]{0:T(1024)} %copy-done.17) | copy-start | bytes 12292
  464.8 148.7 %copy-start.21 = (f32[768]{0:T(1024)S(1)}, f32[768]{0:T(1024)}, u32[]{:S(2)}) copy-start(f32[768]{0:T(1024)} %copy-done.20) | copy-start | bytes 9220
  464.8 148.7 %copy-start.23 = (f32[1024]{0:T(1024)S(1)}, f32[1024]{0:T(1024)}, u32[]{:S(2)}) copy-start(f32[1024]{0:T(1024)} %copy-done.22) | copy-start | bytes 12292
  464.8 148.7 %copy-start.35 = (f32[768]{0:T(1024)S(1)}, f32[768]{0:T(1024)}, u32[]{:S(2)}) copy-start(f32[768]{0:T(1024)} %copy-done.34) | copy-start | bytes 9220
  474.7 6.3 slice-start
  499.4 6.3 slice-start
  617.9 259.7 %reduce-scatter.9.cloned.1.call-start = ((), (), s32[]{:S(2)}) async-start(), calls=%async_computation.13 | async-start | bytes 2506752 | tf_op jit(solution)/shard_map/reduce_scatter | solution.py:278
  622.5 388.0 %reduce-scatter.11.cloned.1.call-start = ((), (), s32[]{:S(2)}) async-start(), calls=%async_computation.14 | async-start | bytes 2506752 | tf_op jit(solution)/shard_map/reduce_scatter | solution.py:279
  625.8 559.9 %reduce-scatter.15.cloned.1.call-start = ((), (), s32[]{:S(2)}) async-start(), calls=%async_computation.16 | async-start | bytes 10027008 | tf_op jit(solution)/shard_map/reduce_scatter | solution.py:281
  636.8 725.4 %reduce-scatter.17.cloned.1.call-start = ((), (), s32[]{:S(2)}) async-start(), calls=%async_computation.17 | async-start | bytes 10027008 | tf_op jit(solution)/shard_map/reduce_scatter | solution.py:282
  646.9 853.9 %all-reduce.25.cloned.1.call-start = ((), (), s32[]{:S(2)}) async-start(), calls=%async_computation.18 | async-start | bytes 1769472 | tf_op jit(solution)/shard_map/psum | solution.py:294
  660.1 746.0 %copy-start.25 = (f32[1024]{0:T(1024)S(1)}, f32[1024]{0:T(1024)}, u32[]{:S(2)}) copy-start(f32[1024]{0:T(1024)} %copy-done.24) | copy-start | bytes 12292
  662.0 744.1 %copy-start.6 = (bf16[1,1024,768]{1,2,0:T(8,128)(2,1)S(1)}, bf16[1,1024,768]{1,2,0:T(8,128)(2,1)}, u32[]{:S(2)}) copy-start(bf16[1,1024,768]{1,2,0:T(8,128)(2,1)} %copy.64) | copy-start | bytes 4718596
  1411.6 86.4 %copy-start.15 = (bf16[1,1024,768]{1,2,0:T(8,128)(2,1)S(1)}, bf16[1,1024,768]{1,2,0:T(8,128)(2,1)}, u32[]{:S(2)}) copy-start(bf16[1,1024,768]{1,2,0:T(8,128)(2,1)} %get-tuple-element.601) | copy-start | bytes 4718596
  (41 other events, 163.2 us)
Sparse Core Ops, SparseCore 0:
  10.8 59.1 all-gather.8
  72.9 54.8 all-gather.6
  130.5 54.9 all-gather.10
  188.2 54.9 all-gather.12
  245.9 79.1 all-gather.14
  327.7 79.2 all-gather.16
  458.2 127.1 reduce-scatter.12
  618.0 127.1 reduce-scatter.6
  750.1 127.4 reduce-scatter.8
  883.1 127.3 reduce-scatter.10
  1016.2 169.3 reduce-scatter.14
  1192.1 170.1 reduce-scatter.16
  1365.6 18.4 all-reduce.24
where the time goes:
time: 1530 us; the launch traced here: 1520 us
  waiting for transfers between devices  841 us (55%)
  matrix products  269 us (18%)
  blocking collectives  197 us (13%)
  local copies, waits for them, and re-layouts  110 us (7%)
  other arithmetic  80 us (5%)
  between operations  17.9 us (1%)
    reduce_scatter x1, waiting for transfers between devices, body(): lax.psum_scatter(grad_outer, 'fsdp', scatter_dimension=1, tiled=True)  175 us
    reduce_scatter x1, waiting for transfers between devices, body(): lax.psum_scatter(grad_inner, 'fsdp', scatter_dimension=1, tiled=True)  174 us
    unnamed x2, blocking collectives  155 us
    reduce_scatter x1, waiting for transfers between devices, body(): lax.psum_scatter(grad_value, 'fsdp', scatter_dimension=1, tiled=True)  131 us
    reduce_scatter x1, waiting for transfers between devices, body(): lax.psum_scatter(grad_key, 'fsdp', scatter_dimension=1, tiled=True)  131 us
    reduce_scatter x1, waiting for transfers between devices, body(): lax.psum_scatter(grad_query, 'fsdp', scatter_dimension=1, tiled=True)  81.5 us
    dot_general x6, matrix products, matmul(): return jnp.dot(operand, matrix, preferred_element_type=jnp.float32)  63.1 us
    all_gather x1, waiting for transfers between devices, body(): lax.all_gather(weight_key, 'fsdp', axis=1, tiled=True)  53.2 us
  transfers between devices with their start and end apart: 13, of which 9 were waited for; matrix products, arithmetic and copies ran while one was open for 25% of the time, Pallas kernels for 0%

commit v1 on v0

--- a/solution.py
+++ b/solution.py
@@ -2,10 +2,836 @@
 
 import jax
 import jax.numpy as jnp
+import numpy as np
 from jax import lax
+from jax.experimental import pallas as pl
+from jax.experimental.pallas import tpu as pltpu
 from jax.sharding import PartitionSpec as P
 
 HD = 64
+BF, F32 = jnp.bfloat16, jnp.float32
+MESH = pl.DeviceIdType.MESH
+SEQ, WIDTH, PIECE, BLOCK = 1024, 768, 48, 256
+EVERY = slice(None)
+
+
+def dg(lhs, rhs, lhs_dim, rhs_dim):
+    return lax.dot_general(
+        lhs, rhs, (((lhs_dim,), (rhs_dim,)), ((), ())), preferred_element_type=F32
+    )
+
+
+def lanes(rows):
+    return lax.broadcasted_iota(jnp.int32, (rows, 128), 1)
+
+
+def aligned(start, size, unit=128):
+    return pl.ds(pl.multiple_of(start, unit), size)
+
+
+class Place:
+    def __init__(self):
+        index = lax.axis_index("fsdp")
+        self.core = lax.axis_index("dp")
+        self.x = lax.rem(index, 2)
+        self.y = lax.rem(lax.div(index, 2), 2)
+        self.z = lax.div(index, 4)
+
+    def at(self, z=None, y=None, x=None, core=None):
+        z = self.z if z is None else z
+        y = self.y if y is None else y
+        x = self.x if x is None else x
+        return (z * 4 + y * 2 + x, self.core if core is None else core)
+
+    def z_after(self, step):
+        return lax.rem(self.z + step, 4)
+
+    def z_peer(self, step):
+        return self.at(z=self.z_after(step))
+
+    def y_peer(self):
+        return self.at(y=1 - self.y)
+
+    def x_peer(self):
+        return self.at(x=1 - self.x)
+
+    def core_peer(self):
+        return self.at(core=1 - self.core)
+
+    def greet(self):
+        ready = pltpu.get_barrier_semaphore()
+        peers = [self.z_peer(1), self.z_peer(2), self.z_peer(3)]
+        peers += [self.y_peer(), self.x_peer(), self.core_peer()]
+        for peer in peers:
+            pl.semaphore_signal(ready, inc=1, device_id=peer, device_id_type=MESH)
+        pl.semaphore_wait(ready, len(peers))
+
+
+class Moves:
+    def __init__(self, send, recv, first):
+        self.send, self.recv, self.first, self.made = send, recv, first, {}
+
+    def add(self, name, src, dst, peer):
+        slot = self.first + len(self.made)
+        self.made[name] = lambda: pltpu.make_async_remote_copy(
+            src_ref=src(),
+            dst_ref=dst(),
+            send_sem=self.send.at[slot],
+            recv_sem=self.recv.at[slot],
+            device_id=peer(),
+            device_id_type=MESH,
+        )
+
+    def start(self, *names):
+        for name in names:
+            self.made[name]().start()
+
+    def landed(self, *names):
+        for name in names:
+            self.made[name]().wait_recv()
+
+    def sent(self):
+        for make in self.made.values():
+            make().wait_send()
+
+
+GATHER_MOVES = 11
+
+
+class Gather(Moves):
+    def __init__(self, me, src, out, local, send, recv, slot, first, half):
+        super().__init__(send, recv, slot * GATHER_MOVES)
+        self.me, self.src, self.out = me, src, out
+        self.local_sem = local.at[slot]
+        cut = half * 2 // 3 if half == 384 else half // 2
+        start = first + me.core * half
+        mine = aligned(start, half)
+        a, b = aligned(start, cut), aligned(start + cut, half - cut)
+        own = lambda: out.at[me.z, me.y, me.x, :, mine]
+        self.mine, self.own = mine, own
+        for step in (1, 2, 3):
+            self.add(("z", step), lambda: src.at[:, mine], own, lambda step=step: me.z_peer(step))
+
+        def same(name, view, peer):
+            self.add(name, view, view, peer)
+
+        same("a1", lambda: out.at[:, me.y, me.x, :, a], me.y_peer)
+        same("b1", lambda: out.at[:, me.y, me.x, :, b], me.x_peer)
+        same("a2", lambda: out.at[:, :, me.x, :, a], me.x_peer)
+        same("b2", lambda: out.at[:, me.y, :, :, b], me.y_peer)
+        same("near a", lambda: out.at[:, :, me.x, :, a], me.core_peer)
+        same("near b", lambda: out.at[:, me.y, :, :, b], me.core_peer)
+        same("far a", lambda: out.at[:, :, 1 - me.x, :, a], me.core_peer)
+        same("far b", lambda: out.at[:, 1 - me.y, :, :, b], me.core_peer)
+
+    def local(self):
+        return pltpu.make_async_copy(self.src.at[:, self.mine], self.own(), self.local_sem)
+
+    def step(self, number):
+        if number == 0:
+            self.start(("z", 2), ("z", 1), ("z", 3))
+            self.local().start()
+        if number == 1:
+            self.local().wait()
+            self.landed(("z", 1), ("z", 2), ("z", 3))
+            self.start("a1", "b1")
+        if number == 2:
+            self.landed("a1", "b1")
+            self.start("a2", "b2", "near a", "near b")
+        if number == 3:
+            self.landed("a2", "b2")
+            self.start("far a", "far b")
+        if number == 4:
+            self.landed("near a", "near b", "far a", "far b")
+            self.sent()
+
+
+class VectorGather(Moves):
+    def __init__(self, me, src, out, local, send, recv, first):
+        super().__init__(send, recv, first)
+        own = lambda: out.at[me.z, me.y, me.x]
+        self.copy = lambda: pltpu.make_async_copy(src, own(), local)
+        for step in (1, 2, 3):
+            self.add(("z", step), lambda: src, own, lambda step=step: me.z_peer(step))
+        self.add("y", lambda: out.at[:, me.y, me.x], lambda: out.at[:, me.y, me.x], me.y_peer)
+        self.add("x", lambda: out.at[:, :, me.x], lambda: out.at[:, :, me.x], me.x_peer)
+
+    def step(self, number):
+        if number == 0:
+            self.copy().start()
+            self.start(("z", 1), ("z", 2), ("z", 3))
+        if number == 1:
+            self.copy().wait()
+            self.landed(("z", 1), ("z", 2), ("z", 3))
+            self.start("y")
+        if number == 2:
+            self.landed("y")
+            self.start("x")
+        if number == 3:
+            self.landed("x")
+            self.sent()
+
+
+REDUCE_MOVES = 9
+
+
+class Reduce(Moves):
+    def __init__(self, me, grads, total, boxes, send, recv, slot, first, half, group):
+        super().__init__(send, recv, slot * REDUCE_MOVES)
+        from_core, from_a1, from_b1, from_a2, from_b2, from_z = boxes
+        self.me, self.grads, self.total, self.boxes = me, grads, total, boxes
+        cut = half * 2 // 3 if half == 384 else half // 2
+        start = first + me.core * half
+        self.half = half
+        self.mine = mine = aligned(start, half)
+        theirs = aligned(first + (1 - me.core) * half, half)
+        self.a, self.b = a, b = aligned(start, cut), aligned(start + cut, half - cut)
+        self.group = group
+        self.add("core", lambda: grads.at[:, :, :, :, theirs], lambda: from_core, me.core_peer)
+        self.add("a1", lambda: grads.at[:, 1 - me.y, :, :, a], lambda: from_a1, me.y_peer)
+        self.add("b1", lambda: grads.at[:, :, 1 - me.x, :, b], lambda: from_b1, me.x_peer)
+        self.add("a2", lambda: grads.at[:, me.y, 1 - me.x, :, a], lambda: from_a2, me.x_peer)
+        self.add("b2", lambda: grads.at[:, 1 - me.y, me.x, :, b], lambda: from_b2, me.y_peer)
+        for step in (1, 2, 3):
+            self.add(
+                ("z", step),
+                lambda step=step: grads.at[me.z_after(step), me.y, me.x, :, mine],
+                lambda step=step: from_z.at[step - 1],
+                lambda step=step: me.z_peer(step),
+            )
+        self.add("last", lambda: total.at[group, :, mine], lambda: total.at[group, :, mine], me.core_peer)
+
+    def step(self, number):
+        me, grads = self.me, self.grads
+        from_core, from_a1, from_b1, from_a2, from_b2, from_z = self.boxes
+        a, b, mine = self.a, self.b, self.mine
+
+        def plus(left, right):
+            return (left.astype(F32) + right.astype(F32)).astype(BF)
+
+        if number == 0:
+            self.start("core")
+        if number == 1:
+            self.landed("core")
+
+            @pl.loop(0, 4)
+            def _(z):
+                for y in range(2):
+                    for x in range(2):
+                        grads[z, y, x, :, mine] = plus(
+                            grads[z, y, x, :, mine], from_core[z, y, x]
+                        )
+
+            self.start("a1", "b1")
+        if number == 2:
+            self.landed("a1", "b1")
+
+            @pl.loop(0, 4)
+            def _(z):
+                for k in range(2):
+                    grads[z, me.y, k, :, a] = plus(grads[z, me.y, k, :, a], from_a1[z, k])
+                    grads[z, k, me.x, :, b] = plus(grads[z, k, me.x, :, b], from_b1[z, k])
+
+            self.start("a2", "b2")
+        if number == 3:
+            self.landed("a2", "b2")
+
+            @pl.loop(0, 4)
+            def _(z):
+                grads[z, me.y, me.x, :, a] = plus(grads[z, me.y, me.x, :, a], from_a2[z])
+                grads[z, me.y, me.x, :, b] = plus(grads[z, me.y, me.x, :, b], from_b2[z])
+
+            self.start(("z", 2), ("z", 1), ("z", 3))
+        if number == 4:
+            self.landed(("z", 1), ("z", 2), ("z", 3))
+            terms = [from_z[k].astype(F32) for k in range(3)]
+            own = grads[me.z, me.y, me.x, :, mine].astype(F32)
+            self.total[self.group, :, mine] = (own + terms[0]) + (terms[1] + terms[2])
+            self.start("last")
+        if number == 5:
+            self.landed("last")
+            self.sent()
+
+
+def boxes_for(half):
+    cut = half * 2 // 3 if half == 384 else half // 2
+    return [
+        pltpu.VMEM((4, 2, 2, PIECE, half), BF),
+        pltpu.VMEM((4, 2, PIECE, cut), BF),
+        pltpu.VMEM((4, 2, PIECE, half - cut), BF),
+        pltpu.VMEM((4, PIECE, cut), BF),
+        pltpu.VMEM((4, PIECE, half - cut), BF),
+        pltpu.VMEM((3, PIECE, half), BF),
+    ]
+
+
+class VectorSum(Moves):
+    def __init__(self, me, table, boxes, send, recv, first):
+        super().__init__(send, recv, first)
+        self.table, self.boxes = table, boxes
+        for k, peer in enumerate((me.core_peer, me.x_peer, me.y_peer)):
+            self.add(k, lambda k=k: table.at[k], lambda k=k: boxes.at[k], peer)
+        for step in (1, 2, 3):
+            self.add(
+                ("z", step),
+                lambda: table.at[3],
+                lambda step=step: boxes.at[2 + step],
+                lambda step=step: me.z_peer(step),
+            )
+
+    def step(self, number):
+        table, boxes = self.table, self.boxes
+        if 1 <= number <= 3:
+            self.landed(number - 1)
+            table[number] = table[number - 1] + boxes[number - 1]
+        if number < 3:
+            self.start(number)
+        if number == 3:
+            self.start(("z", 1), ("z", 2), ("z", 3))
+        if number == 4:
+            self.landed(("z", 1), ("z", 2), ("z", 3))
+            table[4] = (table[3] + boxes[3]) + (boxes[4] + boxes[5])
+            self.sent()
+
+
+def normalized(values):
+    average = jnp.mean(values, axis=-1, keepdims=True)
+    centered = values - average
+    spread = jnp.mean(centered * centered, axis=-1, keepdims=True)
+    scale = lax.rsqrt(spread + 1e-06)
+    return centered * scale, scale
+
+
+def norm_grad(grad_scaled, unit, scale):
+    mean_grad = jnp.mean(grad_scaled, axis=-1, keepdims=True)
+    mean_both = jnp.mean(grad_scaled * unit, axis=-1, keepdims=True)
+    return scale * (grad_scaled - mean_grad - unit * mean_both)
+
+
+def tile_of(whole, group_cols):
+    return whole[:, :, :, :, aligned(group_cols, WIDTH)].reshape(WIDTH, WIDTH)
+
+
+def blocks(count, body):
+    @pl.loop(0, SEQ // count)
+    def _(step):
+        body(aligned(step * count, count, count))
+
+
+N_GATHERS = 8
+FORWARD_SENDS = N_GATHERS * GATHER_MOVES + 5
+
+
+def forward_kernel(
+    tok, seg, sh_qkvo, sh_in, sh_out, pack, pick, rows_of,
+    result, w_qkvo, w_in, w_out, qkv_out, att_out, lse_out, normed_out, mid_out, second_out, act_out, slope_out, vec, stats,
+    b_qkvo, b_in, b_out, got, qkv, att, lse, normed, mid, second, act, slope, res, qa, ka, va, send, recv, local,
+):
+    me = Place()
+    me.greet()
+    vectors = VectorGather(me, pack, got, local.at[8], send, recv, N_GATHERS * GATHER_MOVES)
+    spans = [(sh_qkvo, b_qkvo, 768 * k, 384) for k in range(4)]
+    spans += [(sh_in, b_in, 0, 768), (sh_in, b_in, 1536, 768)]
+    spans += [(sh_out, b_out, 0, 768), (sh_out, b_out, 1536, 768)]
+    chunks = [
+        Gather(me, src, out, local, send, recv, k, first, half)
+        for k, (src, out, first, half) in enumerate(spans)
+    ]
+
+    def tick(number):
+        for k, chunk in enumerate(chunks):
+            if 0 <= number - k <= 4:
+                chunk.step(number - k)
+
+    saves = []
+
+    def save(src, dst):
+        slot = 9 + len(saves)
+        make = lambda: pltpu.make_async_copy(src, dst, local.at[slot])
+        saves.append(make)
+        make().start()
+
+    vectors.step(0)
+    tick(0)
+    vectors.step(1)
+    tick(1)
+    vectors.step(2)
+    tick(2)
+    vectors.step(3)
+    spread = dg(got[...].reshape(256, 128), pick[...], 1, 0)
+    table = jnp.zeros((16, WIDTH), F32)
+    for k in range(16):
+        table += spread[16 * k : 16 * k + 16] * rows_of[k : k + 1]
+    vec[...] = table
+    stats[...] = jnp.zeros_like(stats)
+    lse[...] = jnp.zeros_like(lse)
+
+    def tally(k, piece, valid):
+        stats[k : k + 1] += jnp.sum(piece * piece * valid, axis=0, keepdims=True)
+
+    def valid_of(rows):
+        return jnp.where(seg[rows] != 0, 1.0, 0.0)
+
+    def first_norm(rows):
+        stream = tok[rows].astype(F32)
+        valid = valid_of(rows)
+        tally(0, stream, valid)
+        stats[4:5] += jnp.sum(jnp.broadcast_to(valid, stream.shape), axis=0, keepdims=True)
+        unit, _ = normalized(stream)
+        normed[rows] = (unit * vec[0:1] + vec[1:2]).astype(BF)
+
+    blocks(BLOCK, first_norm)
+    save(normed, normed_out)
+    tick(3)
+    tick(4)
+    tick(5)
+    tick(6)
+    for k, bias in enumerate((2, None, 3)):
+        def project(rows, k=k, bias=bias):
+            made = dg(normed[rows], tile_of(b_qkvo, WIDTH * k), 1, 1)
+            if bias is not None:
+                made = made + vec[bias : bias + 1]
+            qkv[rows, WIDTH * k : WIDTH * k + WIDTH] = made.astype(BF)
+
+        blocks(512, project)
+    tick(7)
+    save(qkv, qkv_out)
+    save(b_qkvo, w_qkvo)
+
+    lane = lanes(SEQ)
+    hot = seg[...] == lane
+    for h in range(2):
+        qa[h, :, 128:] = jnp.where(hot, 1.0, 0.0).astype(BF)
+    ka[:, 128:] = jnp.where(hot | (lane > 8), 0.0, -1e30).astype(BF)
+    va[:, 128:] = jnp.ones((SEQ, 128), BF)
+
+    @pl.loop(0, WIDTH // 128)
+    def _(pair):
+        @pl.when(pair == 2)
+        def _():
+            tick(8)
+
+        @pl.when(pair == 5)
+        def _():
+            tick(9)
+
+        query = qkv[:, aligned(pair * 128, 128)].astype(F32) * 0.125
+        lane = lanes(SEQ)
+        qa[0, :, :128] = jnp.where(lane < 64, query, 0.0).astype(BF)
+        qa[1, :, :128] = jnp.where(lane < 64, 0.0, query).astype(BF)
+        ka[:, :128] = qkv[:, aligned(WIDTH + pair * 128, 128)]
+        va[:, :128] = qkv[:, aligned(2 * WIDTH + pair * 128, 128)]
+        lane = lanes(BLOCK)
+        for step in range(SEQ // BLOCK):
+            rows = slice(step * BLOCK, (step + 1) * BLOCK)
+            mixed = []
+            for h in range(2):
+                scores = dg(qa[h, rows], ka[...], 1, 1)
+                largest = jnp.max(scores, axis=1, keepdims=True)
+                prob = jnp.exp(scores - largest).astype(BF)
+                both = dg(prob, va[...], 1, 0)
+                total = both[:, 128:]
+                mixed.append(both[:, :128] / total)
+                lse[rows] = jnp.where(lane == 2 * pair + h, largest + jnp.log(total), lse[rows])
+            att[rows, aligned(pair * 128, 128)] = jnp.where(lane < 64, mixed[0], mixed[1]).astype(BF)
+
+    save(att, att_out)
+    save(lse, lse_out)
+
+    def second_norm(rows):
+        valid = valid_of(rows)
+        branch = dg(att[rows], tile_of(b_qkvo, 3 * WIDTH), 1, 1) + vec[4:5]
+        middle = tok[rows].astype(F32) + branch
+        tally(1, branch, valid)
+        tally(2, middle, valid)
+        mid[rows] = middle
+        unit, _ = normalized(middle)
+        second[rows] = (unit * vec[6:7] + vec[7:8]).astype(BF)
+
+    blocks(BLOCK, second_norm)
+    save(mid, mid_out)
+    save(second, second_out)
+    save(b_in, w_in)
+    tick(10)
+    for k in range(4):
+        def expand(rows, k=k):
+            cols = slice(k * WIDTH, (k + 1) * WIDTH)
+            hidden = dg(second[rows], tile_of(b_in, k * WIDTH), 1, 1) + vec[8 + k : 9 + k]
+            phi = 0.5 + 0.5 * lax.erf(hidden * (0.5**0.5))
+            bell = jnp.exp(hidden * hidden * -0.5) * 0.3989422804014327
+            act[rows, cols] = (hidden * phi).astype(BF)
+            slope[rows, cols] = (phi + hidden * bell).astype(BF)
+
+        blocks(BLOCK, expand)
+    save(act, act_out)
+    save(slope, slope_out)
+    tick(11)
+    save(b_out, w_out)
+
+    def contract(rows):
+        valid = valid_of(rows)
+        ffn_out = dg(act[rows], b_out[...].reshape(WIDTH, 4 * WIDTH), 1, 1) + vec[5:6]
+        tally(3, ffn_out, valid)
+        res[rows] = (mid[rows] + ffn_out).astype(BF)
+
+    blocks(BLOCK, contract)
+    save(res, result)
+    for make in saves:
+        make().wait()
+
+
+def forward_call(tok, seg, sh_qkvo, sh_in, sh_out, pack):
+    whole = jax.ShapeDtypeStruct((4, 2, 2, PIECE, 4 * WIDTH), BF)
+    wide = lambda k, kind: jax.ShapeDtypeStruct((SEQ, k), kind)
+    outs = [
+        wide(WIDTH, BF), whole, whole, whole, wide(3 * WIDTH, BF), wide(WIDTH, BF), wide(128, F32), wide(WIDTH, BF),
+        wide(WIDTH, F32), wide(WIDTH, BF), wide(4 * WIDTH, BF), wide(4 * WIDTH, BF),
+        jax.ShapeDtypeStruct((16, WIDTH), F32), jax.ShapeDtypeStruct((8, WIDTH), F32),
+    ]
+    vmem, anywhere = pl.BlockSpec(memory_space=pltpu.VMEM), pl.BlockSpec(memory_space=pl.ANY)
+    spot = lambda shape: pltpu.VMEM(shape.shape, shape.dtype)
+    scratch = [spot(whole)] * 3 + [pltpu.VMEM((4, 2, 2, 16, 128), BF)]
+    scratch += [spot(shape) for shape in outs[4:5] + outs[5:6] + outs[6:7] + outs[7:8] + outs[8:12]]
+    scratch += [spot(outs[0]), pltpu.VMEM((2, SEQ, 256), BF), pltpu.VMEM((SEQ, 256), BF), pltpu.VMEM((SEQ, 256), BF)]
+    scratch += [pltpu.SemaphoreType.DMA((FORWARD_SENDS,))] * 2 + [pltpu.SemaphoreType.DMA((22,))]
+    place = np.arange(WIDTH)
+    pick = jnp.asarray((place[None, :] % PIECE == np.arange(128)[:, None]), BF)
+    rows_of = jnp.asarray((place[None, :] // PIECE == np.arange(16)[:, None]), F32)
+    return pl.pallas_call(
+        forward_kernel,
+        out_shape=outs,
+        in_specs=[vmem] * 8,
+        out_specs=[anywhere] * 12 + [vmem] * 2,
+        scratch_shapes=scratch,
+        compiler_params=pltpu.CompilerParams(
+            collective_id=1, has_side_effects=True, vmem_limit_bytes=60 * 2**20
+        ),
+        name="forward",
+    )(tok, seg, sh_qkvo, sh_in, sh_out, pack, pick, rows_of)
+
+
+def packed_inputs(
+    weight_query, weight_key, weight_value, weight_output, weight_inner, weight_outer,
+    bias_query, bias_value, bias_output, bias_inner, bias_outer, gain_attn, shift_attn, gain_ffn, shift_ffn,
+):
+    four = (weight_query, weight_key, weight_value, weight_output)
+    sh_qkvo = jnp.concatenate([w.T for w in four], axis=1)
+    sh_in = weight_inner.T.reshape(4, PIECE, WIDTH).transpose(1, 0, 2).reshape(PIECE, 4 * WIDTH)
+    sh_out = weight_outer.T.reshape(PIECE, 16, 4, PIECE).transpose(0, 2, 1, 3).reshape(PIECE, 4 * WIDTH)
+    vectors = (gain_attn, shift_attn, bias_query, bias_value, bias_output, bias_outer, gain_ffn, shift_ffn)
+    pack = jnp.concatenate([jnp.stack(vectors), bias_inner.reshape(4, PIECE)])
+    pack = jnp.pad(pack, ((0, 4), (0, 128 - PIECE)))
+    return sh_qkvo, sh_in, sh_out, pack
+
+
+N_REDUCES = 8
+BACKWARD_SENDS = N_REDUCES * REDUCE_MOVES + 6
+
+
+def three_terms(values, lane, first, rest):
+    high = values.astype(BF).astype(F32)
+    left = values - high
+    middle = left.astype(BF).astype(F32)
+    low = left - middle
+    for k, term in enumerate((high, middle, low)):
+        rest = jnp.where(lane == first + k, term, rest)
+    return rest.astype(BF)
+
+
+def backward_kernel(
+    tok, cot, seg, vec, stats, w_qkvo, w_in, w_out, qkv_in, att_in, lse_in, normed_in, mid_in, second_in, act_in, slope_in,
+    grad_tok, total, sums,
+    big_a, big_b, first, middle, last, small_a, small_b, mid, lse, qa, ka, va, da, acc, table, tables, send, recv, local, *boxes,
+):
+    me = Place()
+    me.greet()
+    spans = [(last, 0, 768, 2), (last, 1536, 768, 2), (middle, 0, 768, 1), (middle, 1536, 768, 1)]
+    spans += [(first, 2304, 384, 0)] + [(first, 768 * k, 384, 0) for k in range(3)]
+    chunks = [
+        Reduce(me, grads, total, boxes[6 * k : 6 * k + 6], send, recv, k, start, half, group)
+        for k, (grads, start, half, group) in enumerate(spans)
+    ]
+    vectors = VectorSum(me, table, tables, send, recv, N_REDUCES * REDUCE_MOVES)
+    u01, u23, i01, i23, out, que, key, val = chunks
+
+    def load(slot, src, dst):
+        make = lambda: pltpu.make_async_copy(src(), dst(), local.at[slot])
+        make().start()
+        return make
+
+    act_here = load(0, lambda: act_in, lambda: big_a)
+    w_out_here = load(1, lambda: w_out, lambda: first)
+    slope_here = load(2, lambda: slope_in, lambda: big_b)
+    w_in_here = load(3, lambda: w_in, lambda: middle)
+    mid_here = load(4, lambda: mid_in, lambda: mid)
+    second_here = load(5, lambda: second_in, lambda: small_a)
+    att_here = load(6, lambda: att_in, lambda: small_b)
+    lse_here = load(7, lambda: lse_in, lambda: lse)
+
+    sums_ref = table.at[0]
+    sums_ref[...] = jnp.zeros_like(sums_ref)
+    sums_ref[12:20] = stats[...]
+
+    def tally(row, values):
+        sums_ref[row : row + 1] += jnp.sum(values, axis=0, keepdims=True)
+
+    def piece(k):
+        return slice(k * WIDTH, (k + 1) * WIDTH)
+
+    def store_grad(whole, k, left, right):
+        made = dg(left, right, 0, 0).astype(BF)
+        whole[:, :, :, :, piece(k)] = made.reshape(4, 2, 2, PIECE, WIDTH)
+
+    act_here().wait()
+    store_grad(last, 0, cot[...], big_a[:, piece(0)])
+    store_grad(last, 1, cot[...], big_a[:, piece(1)])
+    u01.step(0)
+    store_grad(last, 2, cot[...], big_a[:, piece(2)])
+    store_grad(last, 3, cot[...], big_a[:, piece(3)])
+    u01.step(1)
+    u23.step(0)
+    qkv_here = load(8, lambda: qkv_in, lambda: big_a.at[:, 0 : 3 * WIDTH])
+    w_out_here().wait()
+    slope_here().wait()
+    for k in range(4):
+        def through_gelu(rows, k=k):
+            grad_active = dg(cot[rows], tile_of(first, k * WIDTH), 1, 0)
+            grad_hidden = (grad_active * big_b[rows, piece(k)].astype(F32)).astype(BF)
+            big_b[rows, piece(k)] = grad_hidden
+            tally(8 + k, grad_hidden.astype(F32))
+
+        blocks(BLOCK, through_gelu)
+    u01.step(2)
+    u23.step(1)
+    o_cols = slice(3 * WIDTH, 4 * WIDTH)
+    w_o_here = load(
+        9, lambda: w_qkvo.at[:, :, :, :, o_cols], lambda: first.at[:, :, :, :, o_cols]
+    )
+    w_in_here().wait()
+    mid_here().wait()
+
+    def ffn_norm_back(rows):
+        grad_second = dg(big_b[rows, piece(0)], tile_of(middle, 0), 1, 0)
+        for k in range(1, 4):
+            grad_second += dg(big_b[rows, piece(k)], tile_of(middle, k * WIDTH), 1, 0)
+        unit, scale = normalized(mid[rows])
+        tally(6, grad_second * unit)
+        tally(7, grad_second)
+        upper = cot[rows].astype(F32)
+        tally(5, upper)
+        grad_middle = upper + norm_grad(grad_second * vec[6:7], unit, scale)
+        mid[rows] = grad_middle
+        tally(4, grad_middle.astype(BF).astype(F32))
+
+    blocks(BLOCK, ffn_norm_back)
+    u01.step(3)
+    u23.step(2)
+    second_here().wait()
+    store_grad(middle, 0, big_b[:, piece(0)], small_a[...])
+    store_grad(middle, 1, big_b[:, piece(1)], small_a[...])
+    i01.step(0)
+    store_grad(middle, 2, big_b[:, piece(2)], small_a[...])
+    store_grad(middle, 3, big_b[:, piece(3)], small_a[...])
+    i01.step(1)
+    i23.step(0)
+    u01.step(4)
+    u23.step(3)
+    tok_here = load(10, lambda: tok, lambda: small_a)
+    normed_here = load(11, lambda: normed_in, lambda: big_b.at[:, o_cols])
+    w_o_here().wait()
+    qkv_here().wait()
+
+    def to_attended(rows):
+        big_a[rows, o_cols] = dg(mid[rows].astype(BF), tile_of(first, 3 * WIDTH), 1, 0).astype(BF)
+
+    blocks(512, to_attended)
+    att_here().wait()
+    store_grad(first, 3, mid[...].astype(BF), small_b[...])
+    u01.step(5)
+    out.step(0)
+    lse_here().wait()
+
+    lane = lanes(SEQ)
+    hot = seg[...] == lane
+    ones = (lane > 8) & (lane < 12)
+    ka[:, 128:] = jnp.where(ones, 1.0, jnp.where(hot | (lane > 8), 0.0, -1e30)).astype(BF)
+    va[:, 128:] = jnp.where(lane < 3, 1.0, 0.0).astype(BF)
+
+    w_qkv_cols = slice(0, 3 * WIDTH)
+    w_qkv_make = lambda: pltpu.make_async_copy(
+        w_qkvo.at[:, :, :, :, w_qkv_cols], last.at[:, :, :, :, w_qkv_cols], local.at[12]
+    )
+
+    @pl.loop(0, WIDTH // 128)
+    def _(pair):
+        @pl.when(pair == 1)
+        def _():
+            u23.step(4)
+            i01.step(2)
+            i23.step(1)
+
+        @pl.when(pair == 2)
+        def _():
+            u23.step(5)
+            w_qkv_make().start()
+            i01.step(3)
+            i23.step(2)
+            out.step(1)
+
+        @pl.when(pair == 3)
+        def _():
+            i01.step(4)
+            i23.step(3)
+            out.step(2)
+
+        @pl.when(pair == 4)
+        def _():
+            i01.step(5)
+            i23.step(4)
+            out.step(3)
+
+        @pl.when(pair == 5)
+        def _():
+            i23.step(5)
+            out.step(4)
+
+        spot = pair * 128
+        lane = lanes(SEQ)
+        hot = jnp.where(seg[...] == lane, 1.0, 0.0)
+        query = big_a[:, aligned(spot, 128)].astype(F32) * 0.125
+        ka[:, :128] = big_a[:, aligned(WIDTH + spot, 128)]
+        va[:, :128] = big_a[:, aligned(2 * WIDTH + spot, 128)]
+        upper = big_a[:, aligned(3 * WIDTH + spot, 128)].astype(F32)
+        both = small_b[:, aligned(spot, 128)].astype(F32) * upper
+        for h in range(2):
+            mine = (lane < 64) if h == 0 else (lane >= 64)
+            qa[h, :, :128] = jnp.where(mine, query, 0.0).astype(BF)
+            da[h, :, :128] = jnp.where(mine, upper, 0.0).astype(BF)
+            level = jnp.sum(jnp.where(lane == 2 * pair + h, lse[...], 0.0), axis=1, keepdims=True)
+            qa[h, :, 128:] = three_terms(jnp.broadcast_to(-level, hot.shape), lane, 9, hot)
+            weighted = jnp.sum(jnp.where(mine, both, 0.0), axis=1, keepdims=True)
+            da[h, :, 128:] = three_terms(
+                jnp.broadcast_to(-weighted, hot.shape), lane, 0, jnp.zeros_like(hot)
+            )
+        lane_b = lanes(BLOCK)
+        for step in range(SEQ // BLOCK):
+            rows = slice(step * BLOCK, (step + 1) * BLOCK)
+            for_keys, for_values = [], []
+            for h in range(2):
+                prob = jnp.exp(dg(ka[rows], qa[h], 1, 1))
+                grad_score = (prob * dg(va[rows], da[h], 1, 1)).astype(BF)
+                for_values.append(dg(prob.astype(BF), da[h, :, :128], 1, 0))
+                for_keys.append(dg(grad_score, qa[h, :, :128], 1, 0))
+                for_queries = dg(grad_score, ka[rows, :128], 0, 0)
+                acc[h] = for_queries if step == 0 else acc[h] + for_queries
+            big_b[rows, aligned(WIDTH + spot, 128)] = (for_keys[0] + for_keys[1]).astype(BF)
+            big_b[rows, aligned(2 * WIDTH + spot, 128)] = (for_values[0] + for_values[1]).astype(BF)
+        big_b[:, aligned(spot, 128)] = (jnp.where(lane < 64, acc[0], acc[1]) * 0.125).astype(BF)
+
+    out.step(5)
+    normed_here().wait()
+    store_grad(first, 0, big_b[:, piece(0)], big_b[:, o_cols])
+    que.step(0)
+    store_grad(first, 1, big_b[:, piece(1)], big_b[:, o_cols])
+    que.step(1)
+    key.step(0)
+    store_grad(first, 2, big_b[:, piece(2)], big_b[:, o_cols])
+    key.step(1)
+    val.step(0)
+    tok_here().wait()
+    w_qkv_make().wait()
+
+    @pl.loop(0, SEQ // BLOCK)
+    def _(step):
+        rows = aligned(step * BLOCK, BLOCK, BLOCK)
+        grad_normed = dg(big_b[rows, piece(0)], tile_of(last, 0), 1, 0)
+        for k in range(1, 3):
+            grad_normed += dg(big_b[rows, piece(k)], tile_of(last, k * WIDTH), 1, 0)
+        tally(2, big_b[rows, piece(0)].astype(F32))
+        tally(3, big_b[rows, piece(2)].astype(F32))
+        unit, scale = normalized(small_a[rows].astype(F32))
+        tally(0, grad_normed * unit)
+        tally(1, grad_normed)
+        grad_stream = mid[rows] + norm_grad(grad_normed * vec[0:1], unit, scale)
+        small_b[rows] = grad_stream.astype(BF)
+
+        @pl.when(step == 0)
+        def _():
+            que.step(2)
+            val.step(1)
+
+        @pl.when(step == 2)
+        def _():
+            que.step(3)
+            key.step(2)
+
+    save = load(13, lambda: small_b, lambda: grad_tok)
+    vectors.step(0)
+    val.step(2)
+    key.step(3)
+    vectors.step(1)
+    que.step(4)
+    vectors.step(2)
+    val.step(3)
+    vectors.step(3)
+    key.step(4)
+    que.step(5)
+    vectors.step(4)
+    sums[...] = table[4]
+    val.step(4)
+    key.step(5)
+    val.step(5)
+    save().wait()
+
+
+def backward_call(tok, cot, seg, vec, stats, *kept):
+    vmem, anywhere = pl.BlockSpec(memory_space=pltpu.VMEM), pl.BlockSpec(memory_space=pl.ANY)
+    whole = pltpu.VMEM((4, 2, 2, PIECE, 4 * WIDTH), BF)
+    wide = lambda k, kind: pltpu.VMEM((SEQ, k), kind)
+    scratch = [wide(4 * WIDTH, BF)] * 2 + [whole] * 3 + [wide(WIDTH, BF)] * 2
+    scratch += [wide(WIDTH, F32), wide(128, F32)]
+    scratch += [pltpu.VMEM((2, SEQ, 256), BF), wide(256, BF), wide(256, BF), pltpu.VMEM((2, SEQ, 256), BF)]
+    scratch += [pltpu.VMEM((2, SEQ, 128), F32), pltpu.VMEM((5, 24, WIDTH), F32), pltpu.VMEM((6, 24, WIDTH), F32)]
+    scratch += [pltpu.SemaphoreType.DMA((BACKWARD_SENDS,))] * 2 + [pltpu.SemaphoreType.DMA((14,))]
+    for half in [768] * 4 + [384] * 4:
+        scratch += boxes_for(half)
+    return pl.pallas_call(
+        backward_kernel,
+        out_shape=[
+            jax.ShapeDtypeStruct((SEQ, WIDTH), BF),
+            jax.ShapeDtypeStruct((3, PIECE, 4 * WIDTH), F32),
+            jax.ShapeDtypeStruct((24, WIDTH), F32),
+        ],
+        in_specs=[anywhere] + [vmem] * 4 + [anywhere] * 11,
+        out_specs=[anywhere, vmem, vmem],
+        scratch_shapes=scratch,
+        compiler_params=pltpu.CompilerParams(
+            collective_id=2, has_side_effects=True, vmem_limit_bytes=60 * 2**20
+        ),
+        name="backward",
+    )(tok, cot, seg, vec, stats, *kept)
+
+
+def fast_body(tokens, segment_ids, cotangent, *params):
+    tok, cot = tokens.reshape(SEQ, WIDTH), cotangent.reshape(SEQ, WIDTH)
+    seg = segment_ids.reshape(SEQ, 1)
+    made = forward_call(tok, seg, *packed_inputs(*params))
+    result, kept, vec, stats = made[0], made[1:12], made[12], made[13]
+    grad_tok, total, sums = backward_call(tok, cot, seg, vec, stats, *kept)
+    index = lax.axis_index("fsdp")
+    own = lax.dynamic_slice_in_dim(sums[:12], index * PIECE, PIECE, 1)
+    grad_gain_attn, grad_shift_attn, grad_query, grad_value, grad_output, grad_outer, grad_gain_ffn, grad_shift_ffn = own[:8]
+    grad_inner = own[8:12].reshape(4 * PIECE)
+    squares = jnp.sum(sums[12:16], axis=1)
+    rms_stats = jnp.sqrt(squares / (sums[16, 0] * WIDTH))
+    four = [total[0, :, k * WIDTH : (k + 1) * WIDTH].T for k in range(4)]
+    inner = total[1].reshape(PIECE, 4, WIDTH).transpose(2, 1, 0).reshape(WIDTH, 4 * PIECE)
+    outer = total[2].reshape(PIECE, 4, 16, PIECE).transpose(2, 1, 3, 0).reshape(4 * WIDTH, PIECE)
+    return (
+        result.reshape(tokens.shape), grad_tok.reshape(tokens.shape), *four, inner, outer,
+        grad_query, grad_value, grad_output, grad_inner, grad_outer,
+        grad_gain_attn, grad_shift_attn, grad_gain_ffn, grad_shift_ffn, rms_stats,
+    )
 
 
 def scaled(values, gain_vec):
@@ -126,7 +952,7 @@
     return lax.fori_loop(0, features // pair_width, one_pair, (empty_buf, empty_buf, empty_buf))
 
 
-def body(
+def plain_body(
     tokens,
     segment_ids,
     cotangent,
@@ -371,4 +1197,5 @@
         P("fsdp"),
         P(),
     )
+    body = fast_body if dict(mesh.shape) == {"fsdp": 16, "dp": 2} else plain_body
     return jax.shard_map(body, mesh=mesh, in_specs=in_specs, out_specs=out_specs, check_vma=False)

time: 1530 us -> 266 us (0.17)
  waiting for transfers between devices: 841 us -> 0 us
  matrix products: 269 us -> 0 us
  Pallas kernels: 0 us -> 238 us
  blocking collectives: 197 us -> 0 us
  local copies, waits for them, and re-layouts: 110 us -> 21 us
  other arithmetic: 80 us -> 2.37 us
  between operations: 17.9 us -> 1.79 us
    reduce_scatter x6 -> x0, waiting for transfers between devices: 692 us -> none  [the longest x1 175 us: body(): lax.psum_scatter(grad_outer, 'fsdp', scatter_dimension=1, tiled=True)]
    dot_general x60 -> x0, matrix products: 269 us -> none  [the longest x6 63.1 us: matmul(): return jnp.dot(operand, matrix, preferred_element_type=jnp.float32)]
    pallas_call x0 -> x2, Pallas kernels: none -> 238 us  [the longest x1 129 us: backward_call(): pl.pallas_call(backward_kernel, out_shape=[jax.ShapeDtypeStruct((SEQ, WID...]
    unnamed x2 -> x0, blocking collectives: 155 us -> none
    all_gather x6 -> x0, waiting for transfers between devices: 145 us -> none  [the longest x1 53.2 us: body(): lax.all_gather(weight_key, 'fsdp', axis=1, tiled=True)]
    psum x2 -> x0, blocking collectives: 41.8 us -> none  [the longest x1 39.3 us: body(): square_total, count_total = lax.psum((squares, counted), ('fsdp', 'dp'))]
    convert_element_type x36 -> x0, other arithmetic: 41.2 us -> none  [the longest x6 16.2 us: one_pair(): score_grad = (probability * (prob_grad - weighted)).astype(jnp.bfloat16)]
    dynamic_slice x48 -> x0, local copies, waits for them, and re-layouts: 41.1 us -> none  [the longest x42 36.5 us: pair_of(): lax.dynamic_slice_in_dim(block, offset, 2 * HD, 1).reshape(seq_len, 2, HD)]
  transfers between devices with their start and end apart: 13 -> 0, of which waited for: 9 -> 0; matrix products, arithmetic and copies ran while one was open for 25% -> 0% of each run, Pallas kernels for 0% -> 0%
where the time goes in v1:
time: 266 us; the launch traced here: 263 us
  Pallas kernels  238 us (89%)
  local copies, waits for them, and re-layouts  21 us (8%)
    pallas_call x1, Pallas kernels, backward_call(): pl.pallas_call(backward_kernel, out_shape=[jax.ShapeDtypeStruct((SEQ, WID...  129 us
    pallas_call x1, Pallas kernels, forward_call(): pl.pallas_call(forward_kernel, out_shape=outs, in_specs=[vmem] * 8, out_s...  109 us

profile of v1, /device:TPU:0, one launch (start us, length us, event | category | flops | bytes accessed | tf_op | source)
XLA Modules:
  0.0 263.3 jit_solution(2648743031335500484)
XLA Ops:
  0.7 1.8 copy.44.seg
  2.4 1.7 pad_maximum_fusion.sh_qkvo
  4.1 1.1 copy.42
  5.3 0.7 copy.48
  6.0 0.8 reshape.81
  6.8 0.0 copy-start.12
  6.9 0.0 copy-start.6
  6.9 0.0 copy-start.7
  6.9 0.0 copy-start.10
  6.9 0.2 copy.50
  7.1 2.1 reshape.82.sh_out
  9.2 0.1 reshape.83
  9.4 0.1 concatenate.7
  9.4 0.6 pad.4.pack
  10.0 108.8 %forward.1 = (bf16[1024,768]{1,0:T(8,128)(2,1)}, bf16[4,2,2,48,3072]{4,3,2,1,0:T(8,128)(2,1)}, bf16[4,2,2,48,3072]{4,3,2,1,0:T(8,128)(2,1)}, bf16[4,2,2,48,3072]...) custom-call(bf16[1024,768]{1,0:T(8,128)(2,1)} %bitcast.67, ...), custom_call_target="tpu_custom_call" | custom-call | tf_op jit(solution)/shard_map/forward/pallas_call | solution.py:500
  118.8 129.4 %backward.1 = (bf16[1024,768]{1,0:T(8,128)(2,1)}, f32[3,48,3072]{2,1,0:T(8,128)}, f32[24,768]{1,0:T(8,128)}) custom-call(bf16[1024,768]{1,0:T(8,128)(2,1)} %bitcast.68, bf16[1024,768]{1,0:T(8,128)(2,1)} %bitcast.72, s32[1024,1]{1,0:T(8,128)} %copy.44.seg, f32[16,768]{1,0:T(8,128)} %get-tuple-element.36.vec, f32[8,768]{1,0:T(8,128)} %get-tuple-element.37.stats, ...), custom_call_target="tpu_custom_call" | custom-call | tf_op jit(solution)/shard_map/backward/pallas_call | solution.py:798
  248.2 1.9 slice_bitcast_fusion
  250.2 1.3 fusion
  251.5 0.3 reshape_squeeze.6
  251.8 0.9 copy.46
  252.7 0.7 reshape_squeeze.7
  253.4 0.7 copy.47
  254.1 2.6 %reshape.88 = f32[3072,48]{0,1:T(8,128)} reshape(f32[16,4,48,48]{2,1,0,3:T(4,128)S(1)} %copy.47) | data formatting | bytes 1179648 | tf_op jit(solution)/shard_map/reshape | solution.py:829
  256.8 0.6 dynamic-slice_bitcast_fusion
  257.4 0.1 dynamic-slice.3
  257.4 0.6 reshape.89
  258.1 0.1 slice_reduce_fusion
  258.2 0.5 slice.48
  259.4 0.5 divide_sqrt_fusion
  259.9 1.1 copy.53
  261.1 0.8 copy-done.1
  261.9 1.1 copy.54
  (22 shorter events, 0.1 us)
Async XLA Ops:
  0.7 5.4 %copy-start.2 = (bf16[3072,48]{0,1:T(8,128)(2,1)S(1)}, bf16[3072,48]{0,1:T(8,128)(2,1)}, u32[]{:S(2)}) copy-start(bf16[3072,48]{0,1:T(8,128)(2,1)} %param.28) | copy-start | bytes 884740
  6.8 2.4 copy-start.12
  6.8 2.5 copy-start.4
  6.8 2.5 copy-start.5
  6.9 2.5 copy-start.6
  6.9 2.4 copy-start.7
  6.9 2.4 copy-start.8
  6.9 2.4 copy-start.9
  6.9 2.4 copy-start.10
  6.9 2.4 copy-start.11
  254.1 2.7 %copy-start.3 = (f32[24,768]{1,0:T(8,128)S(1)}, f32[24,768]{1,0:T(8,128)}, u32[]{:S(2)}) copy-start(f32[24,768]{1,0:T(8,128)} %get-tuple-element.51) | copy-start | bytes 221188
  254.1 5.8 %copy-start = (bf16[1024,768]{1,0:T(8,128)(2,1)S(1)}, bf16[1024,768]{1,0:T(8,128)(2,1)}, u32[]{:S(2)}) copy-start(bf16[1024,768]{1,0:T(8,128)(2,1)} %get-tuple-element.35) | copy-start | bytes 4718596
  259.9 2.0 copy-start.1
